TPU v7x, 128 devices: a whole 4x4x4 slice. The times are simulated.
128 devices in a mesh: row: 16 (over x, y), col: 8 (over z, core).
Axes of the slice: x: 4, y: 4, z: 4, core: 2. Of those that a mesh axis runs over, the one named last changes fastest.
Arguments:
- source_points: bfloat16 [65536, 1024], P('row'), may hold values from -8 to 8
- target_points: bfloat16 [32768, 1024], P('col', 'row'), may hold values from -8 to 8
- source_mass: float32 [65536], P('row'), may hold values from 0.25 to 4
- target_mass: float32 [32768], P('col'), may hold values from 0.25 to 4
- tile_index: int32 [256, 16], P('row', 'col'), may hold values from 0 to 15, as said below
- tile_count: int32 [256, 8], P('row', 'col'), may hold values from 1 to 2, as said below
Outputs:
- source_potential: float32 [65536], P('row')
- target_potential: float32 [32768], P('col')
Inputs may be any that keep to these rules, and one draw needn't show every extreme that they name: `tile_index`: within the 2 slots of one source tile and one index of col the target tiles are distinct; every target tile is named by a live slot of some source tile. `tile_count`: each index of row holds, for every index of col, a source tile with all 2 slots live.
All inputs are finite; a program needn't handle non-finite values.
Results may differ from a plain program's by a relative error of at most 0.0003.
Values may be sent and summed in bfloat16 or wider, within the bound.
A program may use at most 128 MiB of HBM per device.

v0:
```python
import math
import jax
import jax.numpy as jnp
from jax import lax
from jax.sharding import PartitionSpec as P

TILE = 256
ITERS = 3
masked_score = -1e30


def cost_terms(piece, source_points, tile_index):
    width = piece.shape[1]
    source_tiles = source_points.reshape(-1, TILE, width)
    target_tiles = piece.reshape(-1, TILE, width)
    chosen = target_tiles[tile_index]
    return jnp.einsum("rad,rkbd->rkab", source_tiles, chosen, preferred_element_type=jnp.float32)


def on_device(source_points, target_points, source_mass, target_mass, tile_index, tile_count):
    tiles_per_row = source_points.shape[0] // TILE
    col_tiles = target_points.shape[0] // TILE
    slot_count = tile_index.shape[1]
    scale = 1.0 / math.sqrt(source_points.shape[1])
    live = jnp.arange(slot_count)[None, :] < tile_count
    onehot = (tile_index[:, :, None] == jnp.arange(col_tiles)[None, None, :]) & live[:, :, None]
    log_source = jnp.log(source_mass).reshape(tiles_per_row, TILE)
    log_target = jnp.log(target_mass).reshape(col_tiles, TILE)
    target_pot = jnp.zeros((col_tiles, TILE), jnp.float32)
    source_pot = jnp.zeros((tiles_per_row, TILE), jnp.float32)
    for iteration in range(ITERS):
        cost = (
            cost_terms(
                lax.all_gather(target_points, "row", axis=1, tiled=True), source_points, tile_index
            )
            * scale
        )
        scores = cost + target_pot[tile_index][:, :, None, :]
        scores = jnp.where(live[:, :, None, None], scores, masked_score)
        row_top = jnp.max(scores, axis=(1, 3))
        highest = lax.pmax(row_top, "col")
        local_sum = jnp.sum(jnp.exp(scores - highest[:, None, :, None]), axis=(1, 3))
        total = lax.psum(local_sum, "col")
        source_pot = log_source - highest - jnp.log(total)
        columns = cost + source_pot[:, None, :, None]
        columns = jnp.where(live[:, :, None, None], columns, masked_score)
        slot_top = jnp.max(columns, axis=2)
        local_top = jnp.max(
            jnp.where(onehot[..., None], slot_top[:, :, None, :], masked_score), axis=(0, 1)
        )
        col_high = lax.pmax(local_top, "row")
        slot_ref = col_high[tile_index]
        sums = jnp.sum(jnp.exp(columns - slot_ref[:, :, None, :]), axis=2)
        col_sum = jnp.sum(jnp.where(onehot[..., None], sums[:, :, None, :], 0.0), axis=(0, 1))
        col_total = lax.psum(col_sum, "row")
        target_pot = log_target - col_high - jnp.log(col_total)
    return (source_pot.reshape(-1), target_pot.reshape(-1))


def solution(mesh):
    placed = (P("row", None), P("col", "row"), P("row"), P("col"), P("row", "col"), P("row", "col"))
    return jax.shard_map(
        on_device, mesh=mesh, in_specs=placed, out_specs=(P("row"), P("col")), check_vma=False
    )
```

profile of v0, /device:TPU:0, one launch (start us, length us, event | category | flops | bytes accessed | tf_op | source)
XLA Modules:
  0.0 747.5 jit_solution(9227641684370280702)
XLA Ops:
  7.2 0.0 all-gather.2.cloned.1.call-start
  7.2 0.7 all-gather.2.cloned.1.call-update
  7.9 0.8 copy.16
  8.7 0.7 compare_select_fusion
  9.3 0.1 copy.15
  9.4 0.1 reshape.101
  9.5 0.6 gather_fusion.1
  10.2 0.7 log.24
  10.9 0.7 log.25
  11.6 0.7 iota_compare_fusion
  12.4 0.1 compare_and_fusion
  12.5 70.8 %all-gather.2.cloned.1.call-done = bf16[4096,1024]{0,1:T(8,128)(2,1)} async-done(((bf16[4096,64]{0,1:T(8,128)(2,1)}), bf16[4096,1024]{0,1:T(8,128)(2,1)}) %all-gather.2.cloned.1.call-update) | async-done | bytes 8388624 | tf_op jit(solution)/shard_map/all_gather | solution.py:34
  83.2 12.0 %copy.14 = bf16[4096,1024]{1,0:T(8,128)(2,1)} copy(bf16[4096,1024]{0,1:T(8,128)(2,1)} %all-gather.2.cloned.1.call-done) | data formatting | bytes 16777216 | tf_op jit(solution)/shard_map/all_gather | solution.py:34
  95.2 10.6 %gather_fusion = bf16[32,256,1024]{2,1,0:T(8,128)(2,1)} fusion(bf16[16,256,1024]{2,1,0:T(8,128)(2,1)} %bitcast.57, s32[1024]{0:T(1024)S(1)} %pad_clamp_fusion), kind=kCustom, calls=%fused_computation | custom fusion | bytes 33554560 | tf_op jit(solution)/shard_map/gather | solution.py:16
  105.8 13.5 %bitcast_reduce_fusion.5 = (f32[16,256]{1,0:T(8,128)S(1)}, f32[16,2,256,256]{3,2,1,0:T(8,128)}) fusion(f32[16,2,256]{2,1,0:T(2,128)S(1)} %reshape.108, pred[16,2]{1,0:T(8,128)(4,1)S(1)} %iota_compare_fusion, bf16[16,2,256,1024]{3,2,1,0:T(8,128)(2,1)} %bitcast.58, bf16[16,256,1024,1]{2,1,3,0:T(8,128)(2,1)} %bitcast.63), kind=kOutput, calls=%fused_computation.28 | convolution fusion | flops 4303351808 | bytes 33603616 | tf_op jit(solution)/shard_map/rad,rkbd->rkab/dot_general | solution.py:17
  119.3 25.8 %pmax.42 = f32[16,256]{1,0:T(8,128)S(1)} all-reduce(f32[16,256]{1,0:T(8,128)S(1)} %get-tuple-element.2), channel_id=1, replica_groups=mesh['row'=16,'col'=8] {'col'}, use_global_device_ids=true, to_apply=%region_1.2 | all-reduce | flops 4096 | bytes 32768 | tf_op jit(solution)/shard_map/pmax | solution.py:41
  145.1 4.6 fusion.11
  149.8 23.6 %psum.42 = f32[16,256]{1,0:T(8,128)S(1)} all-reduce(f32[16,256]{1,0:T(8,128)S(1)} %fusion.11), channel_id=1, replica_groups=mesh['row'=16,'col'=8] {'col'}, use_global_device_ids=true, to_apply=%region_3.4 | all-reduce | flops 4096 | bytes 32768 | tf_op jit(solution)/shard_map/psum | solution.py:43
  173.3 4.7 bitcast_reduce_fusion.4
  178.0 0.1 select_reduce_fusion.5
  178.1 72.4 %pmax.43 = f32[16,256]{1,0:T(8,128)S(1)} all-reduce(f32[16,256]{1,0:T(8,128)S(1)} %select_reduce_fusion.5), channel_id=1, replica_groups=mesh['row'=16,'col'=8] {'row'}, use_global_device_ids=true, to_apply=%region_6.7 | all-reduce | flops 4096 | bytes 32768 | tf_op jit(solution)/shard_map/pmax | solution.py:51
  250.5 0.6 gather_fusion.2
  251.1 5.1 fusion.9
  256.3 0.1 select_reduce_fusion.4
  256.4 69.5 %psum.43 = f32[16,256]{1,0:T(8,128)S(1)} all-reduce(f32[16,256]{1,0:T(8,128)S(1)} %select_reduce_fusion.4), channel_id=1, replica_groups=mesh['row'=16,'col'=8] {'row'}, use_global_device_ids=true, to_apply=%region_9.10 | all-reduce | flops 4096 | bytes 32768 | tf_op jit(solution)/shard_map/psum | solution.py:55
  326.0 0.6 gather_fusion.3
  326.6 4.4 bitcast_reduce_fusion.3
  331.0 23.7 %pmax.44 = f32[16,256]{1,0:T(8,128)S(1)} all-reduce(f32[16,256]{1,0:T(8,128)S(1)} %bitcast_reduce_fusion.3), channel_id=1, replica_groups=mesh['row'=16,'col'=8] {'col'}, use_global_device_ids=true, to_apply=%region_11.12 | all-reduce | flops 4096 | bytes 32768 | tf_op jit(solution)/shard_map/pmax | solution.py:41
  354.8 4.6 fusion.7
  359.4 23.6 %psum.44 = f32[16,256]{1,0:T(8,128)S(1)} all-reduce(f32[16,256]{1,0:T(8,128)S(1)} %fusion.7), channel_id=1, replica_groups=mesh['row'=16,'col'=8] {'col'}, use_global_device_ids=true, to_apply=%region_13.14 | all-reduce | flops 4096 | bytes 32768 | tf_op jit(solution)/shard_map/psum | solution.py:43
  383.0 4.7 bitcast_reduce_fusion.2
  387.6 0.1 select_reduce_fusion.3
  387.8 69.5 %pmax.45 = f32[16,256]{1,0:T(8,128)S(1)} all-reduce(f32[16,256]{1,0:T(8,128)S(1)} %select_reduce_fusion.3), channel_id=1, replica_groups=mesh['row'=16,'col'=8] {'row'}, use_global_device_ids=true, to_apply=%region_16.17 | all-reduce | flops 4096 | bytes 32768 | tf_op jit(solution)/shard_map/pmax | solution.py:51
  457.3 0.6 gather_fusion.4
  458.0 5.1 fusion.5
  463.1 0.1 select_reduce_fusion.2
  463.2 69.5 %psum.45 = f32[16,256]{1,0:T(8,128)S(1)} all-reduce(f32[16,256]{1,0:T(8,128)S(1)} %select_reduce_fusion.2), channel_id=1, replica_groups=mesh['row'=16,'col'=8] {'row'}, use_global_device_ids=true, to_apply=%region_19.20 | all-reduce | flops 4096 | bytes 32768 | tf_op jit(solution)/shard_map/psum | solution.py:55
  532.8 0.6 gather_fusion.5
  533.4 4.4 bitcast_reduce_fusion.1
  537.8 23.6 %pmax.46 = f32[16,256]{1,0:T(8,128)S(1)} all-reduce(f32[16,256]{1,0:T(8,128)S(1)} %bitcast_reduce_fusion.1), channel_id=1, replica_groups=mesh['row'=16,'col'=8] {'col'}, use_global_device_ids=true, to_apply=%region_21.22 | all-reduce | flops 4096 | bytes 32768 | tf_op jit(solution)/shard_map/pmax | solution.py:41
  561.4 4.6 fusion.3
  566.0 23.6 %psum.46 = f32[16,256]{1,0:T(8,128)S(1)} all-reduce(f32[16,256]{1,0:T(8,128)S(1)} %fusion.3), channel_id=1, replica_groups=mesh['row'=16,'col'=8] {'col'}, use_global_device_ids=true, to_apply=%region_23.24 | all-reduce | flops 4096 | bytes 32768 | tf_op jit(solution)/shard_map/psum | solution.py:43
  589.6 4.7 bitcast_reduce_fusion
  594.3 0.1 select_reduce_fusion.1
  594.4 69.5 %pmax.47 = f32[16,256]{1,0:T(8,128)S(1)} all-reduce(f32[16,256]{1,0:T(8,128)S(1)} %select_reduce_fusion.1), channel_id=1, replica_groups=mesh['row'=16,'col'=8] {'row'}, use_global_device_ids=true, to_apply=%region_26.27 | all-reduce | flops 4096 | bytes 32768 | tf_op jit(solution)/shard_map/pmax | solution.py:51
  663.9 0.6 gather_fusion.6
  664.6 5.1 fusion.1
  669.7 0.1 select_reduce_fusion
  669.8 69.5 %psum.47 = f32[16,256]{1,0:T(8,128)S(1)} all-reduce(f32[16,256]{1,0:T(8,128)S(1)} %select_reduce_fusion), channel_id=1, replica_groups=mesh['row'=16,'col'=8] {'row'}, use_global_device_ids=true, to_apply=%region_29.30 | all-reduce | flops 4096 | bytes 32768 | tf_op jit(solution)/shard_map/psum | solution.py:55
  739.4 0.6 copy.19
  740.0 0.6 copy.18
  (16 shorter events, 0.2 us)
Async XLA Ops:
  7.2 76.1 %all-gather.2.cloned.1.call-start = ((), (), s32[]{:S(2)}) async-start(), calls=%async_computation | async-start | bytes 8912896 | tf_op jit(solution)/shard_map/all_gather | solution.py:34
Sparse Core Ops, SparseCore 0:
  10.1 73.0 all-gather.1
where the time goes:
time: 748 us; the launch traced here: 747 us
  blocking collectives  564 us (75%)
  waiting for transfers between devices  71.4 us (10%)
  other arithmetic  54.5 us (7%)
  local copies, waits for them, and re-layouts  30 us (4%)
  between operations  14.3 us (2%)
  matrix products  13.5 us (2%)
    pmax x3, blocking collectives, on_device(): col_high = lax.pmax(local_top, 'row')  211 us
    psum x3, blocking collectives, on_device(): col_total = lax.psum(col_sum, 'row')  209 us
    pmax x3, blocking collectives, on_device(): highest = lax.pmax(row_top, 'col')  73.1 us
    all_gather x1, waiting for transfers between devices, on_device(): lax.all_gather(target_points, 'row', axis=1, tiled=True)  70.8 us
    psum x3, blocking collectives, on_device(): total = lax.psum(local_sum, 'col')  70.7 us
    reduce_sum x3, other arithmetic, on_device(): sums = jnp.sum(jnp.exp(columns - slot_ref[:, :, None, :]), axis=2)  15.4 us
  transfers between devices with their start and end apart: 1, of which 1 were waited for; matrix products, arithmetic and copies ran while one was open for 1% of the time, Pallas kernels for 0%

commit v1 on v0

--- a/solution.py
+++ b/solution.py
@@ -7,6 +7,27 @@
 TILE = 256
 ITERS = 3
 masked_score = -1e30
+
+
+def collect(x, axis, dim):
+    size, place, extent = (lax.axis_size(axis), lax.axis_index(axis), x.shape[dim])
+    forward = [(i, (i + 1) % size) for i in range(size)]
+    left = [(i, (i - 1) % size) for i in range(size)]
+    filled = jnp.zeros((*x.shape[:dim], size * extent, *x.shape[dim + 1 :]), x.dtype)
+    filled = lax.dynamic_update_slice_in_dim(filled, x, place * extent, axis=dim)
+    from_left = from_right = x
+    halfway = size // 2
+    for step in range(1, halfway + 1):
+        from_left = lax.ppermute(from_left, axis, forward)
+        filled = lax.dynamic_update_slice_in_dim(
+            filled, from_left, (place - step) % size * extent, axis=dim
+        )
+        if step < size - halfway:
+            from_right = lax.ppermute(from_right, axis, left)
+            filled = lax.dynamic_update_slice_in_dim(
+                filled, from_right, (place + step) % size * extent, axis=dim
+            )
+    return filled
 
 
 def cost_terms(piece, source_points, tile_index):
@@ -29,12 +50,7 @@
     target_pot = jnp.zeros((col_tiles, TILE), jnp.float32)
     source_pot = jnp.zeros((tiles_per_row, TILE), jnp.float32)
     for iteration in range(ITERS):
-        cost = (
-            cost_terms(
-                lax.all_gather(target_points, "row", axis=1, tiled=True), source_points, tile_index
-            )
-            * scale
-        )
+        cost = cost_terms(collect(target_points, "row", 1), source_points, tile_index) * scale
         scores = cost + target_pot[tile_index][:, :, None, :]
         scores = jnp.where(live[:, :, None, None], scores, masked_score)
         row_top = jnp.max(scores, axis=(1, 3))

time: 748 us -> 960 us (1.28); the launches traced: 747 us -> 950 us
  local copies, waits for them, and re-layouts: 30 us -> 216 us
  starting transfers between devices: 0.04 us -> 37.5 us
  between operations: 14.3 us -> 1.65 us
    dynamic_update_slice x0 -> x16, local copies, waits for them, and re-layouts: none -> 175 us  [the longest x8 86.8 us: collect(): lax.dynamic_update_slice_in_dim(filled, from_left, (place - step) % size...]
    all_gather x1 -> x0, waiting for transfers between devices: 70.8 us -> none  [on_device(): lax.all_gather(target_points, 'row', axis=1, tiled=True)]
    ppermute x0 -> x15, waiting for transfers between devices: none -> 62.5 us  [the longest x8 62.5 us: collect(): from_left = lax.ppermute(from_left, axis, forward)]
    ppermute x0 -> x15, starting transfers between devices: none -> 37.5 us  [the longest x7 35.8 us: collect(): from_right = lax.ppermute(from_right, axis, left)]
    ppermute x0 -> x15, local copies, waits for them, and re-layouts: none -> 16.6 us  [the longest x8 9 us: collect(): from_left = lax.ppermute(from_left, axis, forward)]
    all_gather x1 -> x0, local copies, waits for them, and re-layouts: 12 us -> none  [on_device(): lax.all_gather(target_points, 'row', axis=1, tiled=True)]
  transfers between devices with their start and end apart: 1 -> 15, of which waited for: 1 -> 7; matrix products, arithmetic and copies ran while one was open for 1% -> 20% of each run, Pallas kernels for 0% -> 0%
where the time goes in v1:
time: 960 us; the launch traced here: 950 us
  blocking collectives  565 us (59%)
  local copies, waits for them, and re-layouts  216 us (22%)
  waiting for transfers between devices  62.5 us (7%)
  other arithmetic  53.8 us (6%)
  starting transfers between devices  37.5 us (4%)
  matrix products  13.5 us (1%)
    pmax x3, blocking collectives, on_device(): col_high = lax.pmax(local_top, 'row')  214 us
    psum x3, blocking collectives, on_device(): col_total = lax.psum(col_sum, 'row')  209 us
    dynamic_update_slice x8, local copies, waits for them, and re-layouts, collect(): lax.dynamic_update_slice_in_dim(filled, from_left, (place - step) % size...  86.8 us
    dynamic_update_slice x7, local copies, waits for them, and re-layouts, collect(): lax.dynamic_update_slice_in_dim(filled, from_right, (place + step) % size...  77.9 us
    pmax x3, blocking collectives, on_device(): highest = lax.pmax(row_top, 'col')  71.4 us
    psum x3, blocking collectives, on_device(): total = lax.psum(local_sum, 'col')  70.9 us
    ppermute x8, waiting for transfers between devices, collect(): from_left = lax.ppermute(from_left, axis, forward)  62.5 us
    ppermute x7, starting transfers between devices, collect(): from_right = lax.ppermute(from_right, axis, left)  35.8 us
  transfers between devices with their start and end apart: 15, of which 7 were waited for; matrix products, arithmetic and copies ran while one was open for 20% of the time, Pallas kernels for 0%

profile of v1, /device:TPU:0, one launch (start us, length us, event | category | flops | bytes accessed | tf_op | source)
XLA Modules:
  0.0 949.5 jit_solution(14964658838885799941)
XLA Ops:
  0.6 1.7 collective-permute-start
  2.4 3.7 collective-permute-start.1
  6.1 12.1 %collective-permute-done = bf16[4096,64]{0,1:T(8,128)(2,1)S(1)} collective-permute-done((bf16[4096,64]{0,1:T(8,128)(2,1)}, bf16[4096,64]{0,1:T(8,128)(2,1)S(1)}, u32[]{:S(2)}, u32[]{:S(2)}) %collective-permute-start) | collective-permute-done | bytes 524320 | tf_op jit(solution)/shard_map/ppermute | solution.py:21
  18.1 5.3 collective-permute-start.3
  23.5 11.0 %collective-permute-done.2 = bf16[4096,64]{0,1:T(8,128)(2,1)S(1)} collective-permute-done((bf16[4096,64]{0,1:T(8,128)(2,1)S(1)}, bf16[4096,64]{0,1:T(8,128)(2,1)S(1)}, u32[]{:S(2)}, u32[]{:S(2)}) %collective-permute-start.2) | collective-permute-done | bytes 524320 | tf_op jit(solution)/shard_map/ppermute | solution.py:21
  34.5 5.3 collective-permute-start.5
  39.9 10.1 %collective-permute-done.4 = bf16[4096,64]{0,1:T(8,128)(2,1)S(1)} collective-permute-done((bf16[4096,64]{0,1:T(8,128)(2,1)S(1)}, bf16[4096,64]{0,1:T(8,128)(2,1)S(1)}, u32[]{:S(2)}, u32[]{:S(2)}) %collective-permute-start.4) | collective-permute-done | bytes 524320 | tf_op jit(solution)/shard_map/ppermute | solution.py:21
  50.0 5.3 collective-permute-start.7
  55.3 9.2 collective-permute-done.6
  64.5 5.3 collective-permute-start.9
  69.9 8.3 collective-permute-done.8
  78.1 5.3 collective-permute-start.11
  83.5 7.4 collective-permute-done.10
  91.0 1.5 copy.28
  94.3 5.4 collective-permute-start.13
  99.7 4.5 collective-permute-done.12
  106.4 4.3 broadcast.104
  110.7 10.7 %dynamic_update_slice.32 = bf16[4096,1024]{1,0:T(8,128)(2,1)} dynamic-update-slice(bf16[4096,1024]{1,0:T(8,128)(2,1)} %broadcast.104, bf16[4096,64]{1,0:T(8,128)(2,1)S(1)} %copy.28, s32[]{:T(128)} %constant.158.clone.1, s32[]{:T(128)S(6)} %select_n.270) | dynamic-update-slice | bytes 1048580 | tf_op jit(solution)/shard_map/dynamic_update_slice | solution.py:17
  121.6 1.5 copy.29
  123.1 11.0 %dynamic_update_slice.33 = bf16[4096,1024]{1,0:T(8,128)(2,1)} dynamic-update-slice(bf16[4096,1024]{1,0:T(8,128)(2,1)} %dynamic_update_slice.32, bf16[4096,64]{1,0:T(8,128)(2,1)S(1)} %copy.29, s32[]{:T(128)} %constant.158.clone.1, s32[]{:T(128)S(6)} %select_n.272) | dynamic-update-slice | bytes 1048580 | tf_op jit(solution)/shard_map/dynamic_update_slice | solution.py:22
  134.6 11.8 %dynamic_update_slice.34 = bf16[4096,1024]{1,0:T(8,128)(2,1)} dynamic-update-slice(bf16[4096,1024]{1,0:T(8,128)(2,1)} %dynamic_update_slice.33, bf16[4096,64]{1,0:T(8,128)(2,1)S(1)} %copy.30, s32[]{:T(128)} %constant.158.clone.1, s32[]{:T(128)S(6)} %select_n.274) | dynamic-update-slice | bytes 1048580 | tf_op jit(solution)/shard_map/dynamic_update_slice | solution.py:27
  146.9 9.4 dynamic_update_slice.35
  156.3 1.6 copy.32
  157.9 10.2 %dynamic_update_slice.36 = bf16[4096,1024]{1,0:T(8,128)(2,1)} dynamic-update-slice(bf16[4096,1024]{1,0:T(8,128)(2,1)} %dynamic_update_slice.35, bf16[4096,64]{1,0:T(8,128)(2,1)S(1)} %copy.32, s32[]{:T(128)} %constant.158.clone.1, s32[]{:T(128)S(6)} %select_n.278) | dynamic-update-slice | bytes 1048580 | tf_op jit(solution)/shard_map/dynamic_update_slice | solution.py:27
  168.2 1.5 copy.33
  169.7 11.8 %dynamic_update_slice.37 = bf16[4096,1024]{1,0:T(8,128)(2,1)} dynamic-update-slice(bf16[4096,1024]{1,0:T(8,128)(2,1)} %dynamic_update_slice.36, bf16[4096,64]{1,0:T(8,128)(2,1)S(1)} %copy.33, s32[]{:T(128)} %constant.158.clone.1, s32[]{:T(128)S(6)} %select_n.280) | dynamic-update-slice | bytes 1048580 | tf_op jit(solution)/shard_map/dynamic_update_slice | solution.py:22
  181.5 1.5 copy.34
  183.0 11.8 %dynamic_update_slice.38 = bf16[4096,1024]{1,0:T(8,128)(2,1)} dynamic-update-slice(bf16[4096,1024]{1,0:T(8,128)(2,1)} %dynamic_update_slice.37, bf16[4096,64]{1,0:T(8,128)(2,1)S(1)} %copy.34, s32[]{:T(128)} %constant.158.clone.1, s32[]{:T(128)S(6)} %select_n.282) | dynamic-update-slice | bytes 1048580 | tf_op jit(solution)/shard_map/dynamic_update_slice | solution.py:27
  195.2 10.3 %dynamic_update_slice.39 = bf16[4096,1024]{1,0:T(8,128)(2,1)} dynamic-update-slice(bf16[4096,1024]{1,0:T(8,128)(2,1)} %dynamic_update_slice.38, bf16[4096,64]{1,0:T(8,128)(2,1)S(1)} %copy.35, s32[]{:T(128)} %constant.158.clone.1, s32[]{:T(128)S(6)} %select_n.284) | dynamic-update-slice | bytes 1048580 | tf_op jit(solution)/shard_map/dynamic_update_slice | solution.py:22
  206.1 10.3 %dynamic_update_slice.40 = bf16[4096,1024]{1,0:T(8,128)(2,1)} dynamic-update-slice(bf16[4096,1024]{1,0:T(8,128)(2,1)} %dynamic_update_slice.39, bf16[4096,64]{1,0:T(8,128)(2,1)S(1)} %copy.36, s32[]{:T(128)} %constant.158.clone.1, s32[]{:T(128)S(6)} %select_n.286) | dynamic-update-slice | bytes 1048580 | tf_op jit(solution)/shard_map/dynamic_update_slice | solution.py:27
  217.8 11.8 %dynamic_update_slice.41 = bf16[4096,1024]{1,0:T(8,128)(2,1)} dynamic-update-slice(bf16[4096,1024]{1,0:T(8,128)(2,1)} %dynamic_update_slice.40, bf16[4096,64]{1,0:T(8,128)(2,1)S(1)} %copy.37, s32[]{:T(128)} %constant.158.clone.1, s32[]{:T(128)S(6)} %select_n.288) | dynamic-update-slice | bytes 1048580 | tf_op jit(solution)/shard_map/dynamic_update_slice | solution.py:22
  231.1 11.8 %dynamic_update_slice.42 = bf16[4096,1024]{1,0:T(8,128)(2,1)} dynamic-update-slice(bf16[4096,1024]{1,0:T(8,128)(2,1)} %dynamic_update_slice.41, bf16[4096,64]{1,0:T(8,128)(2,1)S(1)} %copy.38, s32[]{:T(128)} %constant.158.clone.1, s32[]{:T(128)S(6)} %select_n.290) | dynamic-update-slice | bytes 1048580 | tf_op jit(solution)/shard_map/dynamic_update_slice | solution.py:27
  244.4 10.3 %dynamic_update_slice.43 = bf16[4096,1024]{1,0:T(8,128)(2,1)} dynamic-update-slice(bf16[4096,1024]{1,0:T(8,128)(2,1)} %dynamic_update_slice.42, bf16[4096,64]{1,0:T(8,128)(2,1)S(1)} %copy.39, s32[]{:T(128)} %constant.158.clone.1, s32[]{:T(128)S(6)} %select_n.292) | dynamic-update-slice | bytes 1048580 | tf_op jit(solution)/shard_map/dynamic_update_slice | solution.py:22
  255.2 10.3 %dynamic_update_slice.44 = bf16[4096,1024]{1,0:T(8,128)(2,1)} dynamic-update-slice(bf16[4096,1024]{1,0:T(8,128)(2,1)} %dynamic_update_slice.43, bf16[4096,64]{1,0:T(8,128)(2,1)S(1)} %copy.40, s32[]{:T(128)} %constant.158.clone.1, s32[]{:T(128)S(6)} %select_n.294) | dynamic-update-slice | bytes 1048580 | tf_op jit(solution)/shard_map/dynamic_update_slice | solution.py:27
  266.0 11.8 %dynamic_update_slice.45 = bf16[4096,1024]{1,0:T(8,128)(2,1)} dynamic-update-slice(bf16[4096,1024]{1,0:T(8,128)(2,1)} %dynamic_update_slice.44, bf16[4096,64]{1,0:T(8,128)(2,1)S(1)} %copy.41, s32[]{:T(128)} %constant.158.clone.1, s32[]{:T(128)S(6)} %select_n.296) | dynamic-update-slice | bytes 1048580 | tf_op jit(solution)/shard_map/dynamic_update_slice | solution.py:22
  277.8 1.5 copy.42
  279.3 11.7 %dynamic_update_slice.46 = bf16[4096,1024]{1,0:T(8,128)(2,1)} dynamic-update-slice(bf16[4096,1024]{1,0:T(8,128)(2,1)} %dynamic_update_slice.45, bf16[4096,64]{1,0:T(8,128)(2,1)S(1)} %copy.42, s32[]{:T(128)} %constant.158.clone.1, s32[]{:T(128)S(6)} %select_n.298) | dynamic-update-slice | bytes 1048580 | tf_op jit(solution)/shard_map/dynamic_update_slice | solution.py:27
  291.1 1.5 copy.43
  292.6 10.4 %dynamic_update_slice.47 = bf16[4096,1024]{1,0:T(8,128)(2,1)} dynamic-update-slice(bf16[4096,1024]{1,0:T(8,128)(2,1)} %dynamic_update_slice.46, bf16[4096,64]{1,0:T(8,128)(2,1)S(1)} %copy.43, s32[]{:T(128)} %constant.158.clone.1, s32[]{:T(128)S(6)} %select_n.300) | dynamic-update-slice | bytes 1048580 | tf_op jit(solution)/shard_map/dynamic_update_slice | solution.py:22
  303.0 10.6 %gather_fusion = bf16[32,256,1024]{2,1,0:T(8,128)(2,1)} fusion(bf16[16,256,1024]{2,1,0:T(8,128)(2,1)} %bitcast.57, s32[1024]{0:T(1024)S(1)} %pad_clamp_fusion), kind=kCustom, calls=%fused_computation | custom fusion | bytes 33554560 | tf_op jit(solution)/shard_map/gather | solution.py:37
  313.7 13.5 %bitcast_reduce_fusion.5 = (f32[16,256]{1,0:T(8,128)S(1)}, f32[16,2,256,256]{3,2,1,0:T(8,128)}) fusion(f32[16,2,256]{2,1,0:T(2,128)S(1)} %reshape.108, pred[16,2]{1,0:T(8,128)(4,1)S(1)} %iota_compare_fusion, bf16[16,2,256,1024]{3,2,1,0:T(8,128)(2,1)} %bitcast.58, bf16[16,256,1024,1]{2,1,3,0:T(8,128)(2,1)} %bitcast.63), kind=kOutput, calls=%fused_computation.28 | convolution fusion | flops 4303351808 | bytes 33603616 | tf_op jit(solution)/shard_map/rad,rkbd->rkab/dot_general | solution.py:38
  327.1 24.3 %pmax.42 = f32[16,256]{1,0:T(8,128)S(1)} all-reduce(f32[16,256]{1,0:T(8,128)S(1)} %get-tuple-element.2), channel_id=1, replica_groups=mesh['row'=16,'col'=8] {'col'}, use_global_device_ids=true, to_apply=%region_1.2 | all-reduce | flops 4096 | bytes 32768 | tf_op jit(solution)/shard_map/pmax | solution.py:57
  351.4 4.6 fusion.11
  356.1 23.6 %psum.42 = f32[16,256]{1,0:T(8,128)S(1)} all-reduce(f32[16,256]{1,0:T(8,128)S(1)} %fusion.11), channel_id=1, replica_groups=mesh['row'=16,'col'=8] {'col'}, use_global_device_ids=true, to_apply=%region_3.4 | all-reduce | flops 4096 | bytes 32768 | tf_op jit(solution)/shard_map/psum | solution.py:59
  379.6 4.7 bitcast_reduce_fusion.4
  384.4 74.7 %pmax.43 = f32[16,256]{1,0:T(8,128)S(1)} all-reduce(f32[16,256]{1,0:T(8,128)S(1)} %select_reduce_fusion.5), channel_id=1, replica_groups=mesh['row'=16,'col'=8] {'row'}, use_global_device_ids=true, to_apply=%region_6.7 | all-reduce | flops 4096 | bytes 32768 | tf_op jit(solution)/shard_map/pmax | solution.py:67
  459.8 5.1 fusion.9
  465.1 69.5 %psum.43 = f32[16,256]{1,0:T(8,128)S(1)} all-reduce(f32[16,256]{1,0:T(8,128)S(1)} %select_reduce_fusion.4), channel_id=1, replica_groups=mesh['row'=16,'col'=8] {'row'}, use_global_device_ids=true, to_apply=%region_9.10 | all-reduce | flops 4096 | bytes 32768 | tf_op jit(solution)/shard_map/psum | solution.py:71
  535.2 4.4 bitcast_reduce_fusion.3
  539.7 23.6 %pmax.44 = f32[16,256]{1,0:T(8,128)S(1)} all-reduce(f32[16,256]{1,0:T(8,128)S(1)} %bitcast_reduce_fusion.3), channel_id=1, replica_groups=mesh['row'=16,'col'=8] {'col'}, use_global_device_ids=true, to_apply=%region_11.12 | all-reduce | flops 4096 | bytes 32768 | tf_op jit(solution)/shard_map/pmax | solution.py:57
  563.2 4.6 fusion.7
  567.9 23.8 %psum.44 = f32[16,256]{1,0:T(8,128)S(1)} all-reduce(f32[16,256]{1,0:T(8,128)S(1)} %fusion.7), channel_id=1, replica_groups=mesh['row'=16,'col'=8] {'col'}, use_global_device_ids=true, to_apply=%region_13.14 | all-reduce | flops 4096 | bytes 32768 | tf_op jit(solution)/shard_map/psum | solution.py:59
  591.7 4.7 bitcast_reduce_fusion.2
  596.5 69.5 %pmax.45 = f32[16,256]{1,0:T(8,128)S(1)} all-reduce(f32[16,256]{1,0:T(8,128)S(1)} %select_reduce_fusion.3), channel_id=1, replica_groups=mesh['row'=16,'col'=8] {'row'}, use_global_device_ids=true, to_apply=%region_16.17 | all-reduce | flops 4096 | bytes 32768 | tf_op jit(solution)/shard_map/pmax | solution.py:67
  666.6 5.1 fusion.5
  671.9 69.5 %psum.45 = f32[16,256]{1,0:T(8,128)S(1)} all-reduce(f32[16,256]{1,0:T(8,128)S(1)} %select_reduce_fusion.2), channel_id=1, replica_groups=mesh['row'=16,'col'=8] {'row'}, use_global_device_ids=true, to_apply=%region_19.20 | all-reduce | flops 4096 | bytes 32768 | tf_op jit(solution)/shard_map/psum | solution.py:71
  742.1 4.4 bitcast_reduce_fusion.1
  746.5 23.6 %pmax.46 = f32[16,256]{1,0:T(8,128)S(1)} all-reduce(f32[16,256]{1,0:T(8,128)S(1)} %bitcast_reduce_fusion.1), channel_id=1, replica_groups=mesh['row'=16,'col'=8] {'col'}, use_global_device_ids=true, to_apply=%region_21.22 | all-reduce | flops 4096 | bytes 32768 | tf_op jit(solution)/shard_map/pmax | solution.py:57
  770.1 4.6 fusion.3
  774.7 23.6 %psum.46 = f32[16,256]{1,0:T(8,128)S(1)} all-reduce(f32[16,256]{1,0:T(8,128)S(1)} %fusion.3), channel_id=1, replica_groups=mesh['row'=16,'col'=8] {'col'}, use_global_device_ids=true, to_apply=%region_23.24 | all-reduce | flops 4096 | bytes 32768 | tf_op jit(solution)/shard_map/psum | solution.py:59
  798.3 4.7 bitcast_reduce_fusion
  803.1 69.5 %pmax.47 = f32[16,256]{1,0:T(8,128)S(1)} all-reduce(f32[16,256]{1,0:T(8,128)S(1)} %select_reduce_fusion.1), channel_id=1, replica_groups=mesh['row'=16,'col'=8] {'row'}, use_global_device_ids=true, to_apply=%region_26.27 | all-reduce | flops 4096 | bytes 32768 | tf_op jit(solution)/shard_map/pmax | solution.py:67
  873.3 5.1 fusion.1
  878.5 69.5 %psum.47 = f32[16,256]{1,0:T(8,128)S(1)} all-reduce(f32[16,256]{1,0:T(8,128)S(1)} %select_reduce_fusion), channel_id=1, replica_groups=mesh['row'=16,'col'=8] {'row'}, use_global_device_ids=true, to_apply=%region_29.30 | all-reduce | flops 4096 | bytes 32768 | tf_op jit(solution)/shard_map/psum | solution.py:71
  (82 shorter events, 16.6 us)
Async XLA Ops:
  0.6 120.8 %copy-start.9 = (s32[16,1]{0,1:T(1,128)S(1)}, s32[16,1]{0,1:T(1,128)}, u32[]{:S(2)}) copy-start(s32[16,1]{0,1:T(1,128)} %param.11) | copy-start | bytes 196
  0.6 17.5 %collective-permute-start = (bf16[4096,64]{0,1:T(8,128)(2,1)}, bf16[4096,64]{0,1:T(8,128)(2,1)S(1)}, u32[]{:S(2)}, u32[]{:S(2)}) collective-permute-start(bf16[4096,64]{0,1:T(8,128)(2,1)} %param.7), channel_id=1, source_target_pairs={{0,8},{8,16},{16,24},{24,32},{32,40},{40,48},{48,56},{56,64},{64,7... | collective-permute-start | bytes 1572872 | tf_op jit(solution)/shard_map/ppermute | solution.py:21
  2.4 15.8 %collective-permute-start.1 = (bf16[4096,64]{0,1:T(8,128)(2,1)}, bf16[4096,64]{0,1:T(8,128)(2,1)S(1)}, u32[]{:S(2)}, u32[]{:S(2)}) collective-permute-start(bf16[4096,64]{0,1:T(8,128)(2,1)} %param.7), channel_id=1, source_target_pairs={{0,120},{8,0},{16,8},{24,16},{32,24},{40,32},{48,40},{56,48},{64,5... | collective-permute-start | bytes 1572872 | tf_op jit(solution)/shard_map/ppermute | solution.py:26
  18.1 65.3 %copy-start = (bf16[4096,64]{0,1:T(8,128)(2,1)}, bf16[4096,64]{0,1:T(8,128)(2,1)S(1)}, u32[]{:S(2)}) copy-start(bf16[4096,64]{0,1:T(8,128)(2,1)S(1)} %collective-permute-done) | copy-start | bytes 1572868
  18.1 16.4 %collective-permute-start.2 = (bf16[4096,64]{0,1:T(8,128)(2,1)S(1)}, bf16[4096,64]{0,1:T(8,128)(2,1)S(1)}, u32[]{:S(2)}, u32[]{:S(2)}) collective-permute-start(bf16[4096,64]{0,1:T(8,128)(2,1)S(1)} %collective-permute-done), channel_id=1, source_target_pairs={{0,8},{8,16},{16,24},{24,32},{32,40},{40,48},{48,56},{56,64},{64,7... | collective-permute-start | bytes 1572872 | tf_op jit(solution)/shard_map/ppermute | solution.py:21
  18.1 16.4 %collective-permute-start.3 = (bf16[4096,64]{0,1:T(8,128)(2,1)S(1)}, bf16[4096,64]{0,1:T(8,128)(2,1)S(1)}, u32[]{:S(2)}, u32[]{:S(2)}) collective-permute-start(bf16[4096,64]{0,1:T(8,128)(2,1)S(1)} %collective-permute-done.1), channel_id=1, source_target_pairs={{0,120},{8,0},{16,8},{24,16},{32,24},{40,32},{48,40},{56,48},{64,5... | collective-permute-start | bytes 1572872 | tf_op jit(solution)/shard_map/ppermute | solution.py:26
  34.5 15.5 %collective-permute-start.4 = (bf16[4096,64]{0,1:T(8,128)(2,1)S(1)}, bf16[4096,64]{0,1:T(8,128)(2,1)S(1)}, u32[]{:S(2)}, u32[]{:S(2)}) collective-permute-start(bf16[4096,64]{0,1:T(8,128)(2,1)S(1)} %collective-permute-done.2), channel_id=1, source_target_pairs={{0,8},{8,16},{16,24},{24,32},{32,40},{40,48},{48,56},{56,64},{64,7... | collective-permute-start | bytes 1572872 | tf_op jit(solution)/shard_map/ppermute | solution.py:21
  34.5 43.6 %copy-start.1 = (bf16[4096,64]{0,1:T(8,128)(2,1)}, bf16[4096,64]{0,1:T(8,128)(2,1)S(1)}, u32[]{:S(2)}) copy-start(bf16[4096,64]{0,1:T(8,128)(2,1)S(1)} %collective-permute-done.3) | copy-start | bytes 1572868
  34.5 15.5 %collective-permute-start.5 = (bf16[4096,64]{0,1:T(8,128)(2,1)S(1)}, bf16[4096,64]{0,1:T(8,128)(2,1)S(1)}, u32[]{:S(2)}, u32[]{:S(2)}) collective-permute-start(bf16[4096,64]{0,1:T(8,128)(2,1)S(1)} %collective-permute-done.3), channel_id=1, source_target_pairs={{0,120},{8,0},{16,8},{24,16},{32,24},{40,32},{48,40},{56,48},{64,5... | collective-permute-start | bytes 1572872 | tf_op jit(solution)/shard_map/ppermute | solution.py:26
  50.0 41.0 %copy-start.2 = (bf16[4096,64]{0,1:T(8,128)(2,1)}, bf16[4096,64]{0,1:T(8,128)(2,1)S(1)}, u32[]{:S(2)}) copy-start(bf16[4096,64]{0,1:T(8,128)(2,1)S(1)} %collective-permute-done.4) | copy-start | bytes 1572868
  50.0 14.5 %collective-permute-start.6 = (bf16[4096,64]{0,1:T(8,128)(2,1)S(1)}, bf16[4096,64]{0,1:T(8,128)(2,1)S(1)}, u32[]{:S(2)}, u32[]{:S(2)}) collective-permute-start(bf16[4096,64]{0,1:T(8,128)(2,1)S(1)} %collective-permute-done.4), channel_id=1, source_target_pairs={{0,8},{8,16},{16,24},{24,32},{32,40},{40,48},{48,56},{56,64},{64,7... | collective-permute-start | bytes 1572872 | tf_op jit(solution)/shard_map/ppermute | solution.py:21
  50.0 41.0 %copy-start.3 = (bf16[4096,64]{0,1:T(8,128)(2,1)}, bf16[4096,64]{0,1:T(8,128)(2,1)S(1)}, u32[]{:S(2)}) copy-start(bf16[4096,64]{0,1:T(8,128)(2,1)S(1)} %collective-permute-done.5) | copy-start | bytes 1572868
  50.0 14.5 %collective-permute-start.7 = (bf16[4096,64]{0,1:T(8,128)(2,1)S(1)}, bf16[4096,64]{0,1:T(8,128)(2,1)S(1)}, u32[]{:S(2)}, u32[]{:S(2)}) collective-permute-start(bf16[4096,64]{0,1:T(8,128)(2,1)S(1)} %collective-permute-done.5), channel_id=1, source_target_pairs={{0,120},{8,0},{16,8},{24,16},{32,24},{40,32},{48,40},{56,48},{64,5... | collective-permute-start | bytes 1572872 | tf_op jit(solution)/shard_map/ppermute | solution.py:26
  64.5 26.4 %copy-start.4 = (bf16[4096,64]{0,1:T(8,128)(2,1)}, bf16[4096,64]{0,1:T(8,128)(2,1)S(1)}, u32[]{:S(2)}) copy-start(bf16[4096,64]{0,1:T(8,128)(2,1)S(1)} %collective-permute-done.6) | copy-start | bytes 1572868
  64.5 13.6 %collective-permute-start.8 = (bf16[4096,64]{0,1:T(8,128)(2,1)S(1)}, bf16[4096,64]{0,1:T(8,128)(2,1)S(1)}, u32[]{:S(2)}, u32[]{:S(2)}) collective-permute-start(bf16[4096,64]{0,1:T(8,128)(2,1)S(1)} %collective-permute-done.6), channel_id=1, source_target_pairs={{0,8},{8,16},{16,24},{24,32},{32,40},{40,48},{48,56},{56,64},{64,7... | collective-permute-start | bytes 1572872 | tf_op jit(solution)/shard_map/ppermute | solution.py:21
  64.5 26.4 %copy-start.6 = (bf16[4096,64]{0,1:T(8,128)(2,1)}, bf16[4096,64]{0,1:T(8,128)(2,1)S(1)}, u32[]{:S(2)}) copy-start(bf16[4096,64]{0,1:T(8,128)(2,1)S(1)} %collective-permute-done.7) | copy-start | bytes 1572868
  64.5 13.6 %collective-permute-start.9 = (bf16[4096,64]{0,1:T(8,128)(2,1)S(1)}, bf16[4096,64]{0,1:T(8,128)(2,1)}, u32[]{:S(2)}, u32[]{:S(2)}) collective-permute-start(bf16[4096,64]{0,1:T(8,128)(2,1)S(1)} %collective-permute-done.7), channel_id=1, source_target_pairs={{0,120},{8,0},{16,8},{24,16},{32,24},{40,32},{48,40},{56,48},{64,5... | collective-permute-start | bytes 1572872 | tf_op jit(solution)/shard_map/ppermute | solution.py:26
  78.1 12.8 %copy-start.8 = (bf16[4096,64]{0,1:T(8,128)(2,1)}, bf16[4096,64]{0,1:T(8,128)(2,1)S(1)}, u32[]{:S(2)}) copy-start(bf16[4096,64]{0,1:T(8,128)(2,1)S(1)} %collective-permute-done.8) | copy-start | bytes 1572868
  78.1 12.8 %collective-permute-start.10 = (bf16[4096,64]{0,1:T(8,128)(2,1)S(1)}, bf16[4096,64]{0,1:T(8,128)(2,1)}, u32[]{:S(2)}, u32[]{:S(2)}) collective-permute-start(bf16[4096,64]{0,1:T(8,128)(2,1)S(1)} %collective-permute-done.8), channel_id=1, source_target_pairs={{0,8},{8,16},{16,24},{24,32},{32,40},{40,48},{48,56},{56,64},{64,7... | collective-permute-start | bytes 1572872 | tf_op jit(solution)/shard_map/ppermute | solution.py:21
  78.1 16.2 %collective-permute-start.11 = (bf16[4096,64]{0,1:T(8,128)(2,1)}, bf16[4096,64]{0,1:T(8,128)(2,1)S(1)}, u32[]{:S(2)}, u32[]{:S(2)}) collective-permute-start(bf16[4096,64]{0,1:T(8,128)(2,1)} %collective-permute-done.9), channel_id=1, source_target_pairs={{0,120},{8,0},{16,8},{24,16},{32,24},{40,32},{48,40},{56,48},{64,5... | collective-permute-start | bytes 1572872 | tf_op jit(solution)/shard_map/ppermute | solution.py:26
  90.9 13.3 %collective-permute-start.12 = (bf16[4096,64]{0,1:T(8,128)(2,1)}, bf16[4096,64]{0,1:T(8,128)(2,1)S(1)}, u32[]{:S(2)}, u32[]{:S(2)}) collective-permute-start(bf16[4096,64]{0,1:T(8,128)(2,1)} %collective-permute-done.10), channel_id=1, source_target_pairs={{0,8},{8,16},{16,24},{24,32},{32,40},{40,48},{48,56},{56,64},{64,7... | collective-permute-start | bytes 1572872 | tf_op jit(solution)/shard_map/ppermute | solution.py:21
  94.3 183.4 %collective-permute-start.13 = (bf16[4096,64]{0,1:T(8,128)(2,1)S(1)}, bf16[4096,64]{0,1:T(8,128)(2,1)}, u32[]{:S(2)}, u32[]{:S(2)}) collective-permute-start(bf16[4096,64]{0,1:T(8,128)(2,1)S(1)} %collective-permute-done.11), channel_id=1, source_target_pairs={{0,120},{8,0},{16,8},{24,16},{32,24},{40,32},{48,40},{56,48},{64,5... | collective-permute-start | bytes 1572872 | tf_op jit(solution)/shard_map/ppermute | solution.py:26
  104.2 186.9 %collective-permute-start.14 = (bf16[4096,64]{0,1:T(8,128)(2,1)S(1)}, bf16[4096,64]{0,1:T(8,128)(2,1)}, u32[]{:S(2)}, u32[]{:S(2)}) collective-permute-start(bf16[4096,64]{0,1:T(8,128)(2,1)S(1)} %collective-permute-done.12), channel_id=1, source_target_pairs={{0,8},{8,16},{16,24},{24,32},{32,40},{40,48},{48,56},{56,64},{64,7... | collective-permute-start | bytes 1572872 | tf_op jit(solution)/shard_map/ppermute | solution.py:21
  156.3 38.5 %copy-start.5 = (bf16[4096,64]{0,1:T(8,128)(2,1)S(1)}, bf16[4096,64]{0,1:T(8,128)(2,1)}, u32[]{:S(2)}) copy-start(bf16[4096,64]{0,1:T(8,128)(2,1)} %copy-done.4) | copy-start | bytes 1572868
  156.3 49.3 %copy-start.7 = (bf16[4096,64]{0,1:T(8,128)(2,1)S(1)}, bf16[4096,64]{0,1:T(8,128)(2,1)}, u32[]{:S(2)}) copy-start(bf16[4096,64]{0,1:T(8,128)(2,1)} %copy-done.6) | copy-start | bytes 1572868
